TPU v7x, 256 devices: a whole 4x4x8 slice. The times are simulated.
256 devices in a mesh: row: 32 (over z, x_hi, core), col: 8 (over y, x_lo).
Axes of the slice: x: 4 (x_hi: 2, x_lo: 2; x = x_hi * 2 + x_lo), y: 4, z: 8, core: 2. Of those that a mesh axis runs over, the one named last changes fastest.
Arguments:
- pair_map: bfloat16 [64, 1024, 1024], P(None, 'row', 'col'), may hold values from -6 to 6
- kernel_one_a: bfloat16 [3, 3, 64, 64], replicated, may hold values from -0.25 to 0.25
- bias_one_a: float32 [64], replicated, may hold values from -3 to 3
- kernel_one_b: bfloat16 [3, 3, 64, 64], replicated, may hold values from -0.25 to 0.25
- bias_one_b: float32 [64], replicated, may hold values from -3 to 3
- kernel_two_a: bfloat16 [3, 3, 64, 64], replicated, may hold values from -0.25 to 0.25
- bias_two_a: float32 [64], replicated, may hold values from -3 to 3
- kernel_two_b: bfloat16 [3, 3, 64, 64], replicated, may hold values from -0.25 to 0.25
- bias_two_b: float32 [64], replicated, may hold values from -3 to 3
Outputs:
- pair_out: bfloat16 [64, 1024, 1024], P(None, 'row', 'col')
All inputs are finite; a program needn't handle non-finite values.
Results may differ from a plain program's by a relative error of at most 0.0064.
Values may be sent and summed in bfloat16 or wider, within the bound.
A program may use at most 64 MiB of HBM per device.

v0:
```python
import functools

import jax
import jax.numpy as jnp
from jax import lax
from jax.experimental import pallas as pl
from jax.experimental.pallas import tpu as pltpu
from jax.sharding import PartitionSpec as P

MESH = pl.DeviceIdType.MESH
F32, BF16 = jnp.float32, jnp.bfloat16
NT = (((1,), (1,)), ((), ()))
ROWS, COLS, CHAN, SIDE, QUAD = 32, 128, 64, 8, 4
ROW_PAD, COL_PAD, HID_ROW, HID_COL = 8, 16, 4, 8
NEIGHBOURS = [(-1, 0), (-1, -1), (-1, 1), (0, -1), (0, 1), (1, -1), (1, 1), (1, 0)]
ORDER = [0, 7, 1, 2, 5, 6, 3, 4]
SIDEWAYS, OTHERS = [3, 4], [0, 7, 1, 2, 5, 6]


def elu(v):
    return jnp.where(v > 0, v, jnp.exp(jnp.minimum(v, 0.0)) - 1.0)


def rounded(v):
    return v.astype(BF16).astype(F32)


def low_lanes(shape):
    return lax.broadcasted_iota(jnp.int32, shape, len(shape) - 1) < CHAN


def doubled(packed):
    turned = pltpu.roll(packed, CHAN, packed.ndim - 1)
    low = low_lanes(packed.shape)
    return jnp.where(low, packed, turned), jnp.where(low, turned, packed)


def paired(first, second):
    return jnp.where(low_lanes(first.shape), first, second)


def nearby(at, step):
    upper = step // 4
    middle = lax.rem(upper + step // 2, 2)
    return (
        lax.rem(at // 4 + upper, 2) * 4
        + lax.rem(at // 2 + middle, 2) * 2
        + lax.rem(at + step, 2)
    )


class Halo:
    def __init__(self, rows, frame, send, recv, send_sem, recv_sem, row, col):
        self.rows, self.frame = rows, frame
        self.send, self.recv = send, recv
        self.send_sem, self.recv_sem = send_sem, recv_sem
        self.row, self.col = row, col

    def parts(self, at):
        dr, dc = NEIGHBOURS[at]
        if dc == 0:
            return 0 if dr < 0 else 1, self.rows * 4
        if dr == 0:
            return 2 if dc < 0 else 3, 8
        return 4 + (dr > 0) * 2 + (dc > 0), self.rows // 4

    def copy(self, at):
        dr, dc = NEIGHBOURS[at]
        there = len(NEIGHBOURS) - 1 - at
        mine, count = self.parts(at)
        other, _ = self.parts(there)
        device = (lax.rem(self.row + dr + 32, 32), lax.rem(self.col + dc + SIDE, SIDE))
        return pltpu.make_async_remote_copy(
            self.send.at[mine, pl.ds(0, count)],
            self.recv.at[other, pl.ds(0, count)],
            self.send_sem.at[mine],
            self.recv_sem.at[other],
            device_id=device,
            device_id_type=MESH,
        )

    def incoming(self, at):
        mine, count = self.parts(at)
        there = self.recv.at[mine, pl.ds(0, count)]
        return pltpu.make_async_copy(there, there, self.recv_sem.at[mine])

    def pack(self, start=False):
        frame, rows = self.frame, self.rows
        for at in ORDER:
            dr, dc = NEIGHBOURS[at]
            mine, _ = self.parts(at)
            top = ROW_PAD if dr < 0 else ROW_PAD + ROWS - rows
            left = COL_PAD if dc < 0 else COL_PAD + COLS - 8
            if dc == 0:

                lines = frame[top : top + rows, COL_PAD : COL_PAD + COLS, :]
                both = paired(lines[:, :64], lines[:, 64:]).astype(BF16)
                self.send[mine, 0 : rows * 4] = both.reshape(rows * 4, 16, 128)
            else:
                base, many = (ROW_PAD, ROWS // 4) if dr == 0 else (top, rows // 4)

                for t in range(many):
                    block = frame[base + 4 * t : base + 4 * t + 4, left : left + 8, :]
                    both = paired(block[:2].reshape(16, 128), block[2:].reshape(16, 128))
                    self.send[mine, t] = both.astype(BF16)
            if start:
                self.copy(at).start()

    def start(self):
        for at in ORDER:
            self.copy(at).start()

    def finish(self, which):
        frame, rows = self.frame, self.rows
        for at in which:
            dr, dc = NEIGHBOURS[at]
            self.incoming(at).wait()
            mine, _ = self.parts(at)
            inside = jnp.logical_and(
                jnp.logical_and(self.row + dr >= 0, self.row + dr < 32),
                jnp.logical_and(self.col + dc >= 0, self.col + dc < SIDE),
            )
            top = ROW_PAD - rows if dr < 0 else ROW_PAD + ROWS
            left = COL_PAD - 8 if dc < 0 else COL_PAD + COLS
            if dc == 0:

                for i in range(rows):
                    line = self.recv[mine, i * 4 : i * 4 + 4].reshape(64, 128).astype(F32)
                    first, second = doubled(jnp.where(inside, line, 0.0))
                    frame[top + i, COL_PAD : COL_PAD + 64, :] = first
                    frame[top + i, COL_PAD + 64 : COL_PAD + 128, :] = second
            else:
                base, many = (ROW_PAD, ROWS // 4) if dr == 0 else (top, rows // 4)

                for t in range(many):
                    block = self.recv[mine, t].astype(F32)
                    first, second = doubled(jnp.where(inside, block, 0.0))
                    i = base + 4 * t
                    frame[i : i + 2, left : left + 8, :] = first.reshape(2, 8, 128)
                    frame[i + 2 : i + 4, left : left + 8, :] = second.reshape(2, 8, 128)
        for at in which:
            self.copy(at).wait_send()


def three_taps(kernel, ky, swapped=False):
    pick = lambda kx: kernel[kx, ky] if swapped else kernel[ky, kx]
    zeros = jnp.zeros((CHAN, CHAN), BF16)
    return jnp.concatenate([pick(0), pick(1), pick(2), zeros], axis=1)


def body(
    x_hbm, k1a_hbm, b1a_hbm, k1b_hbm, b1b_hbm, k2a_hbm, b2a_hbm, k2b_hbm, b2b_hbm, out_ref,
    x_ref, k1a, k1b, k2a, k2b, b1a, b1b, b2a, b2b, load_sem, flat, frame, slab, hidden, wide, block_y, outbox, transit, inbox,
    halo_send, halo_recv, w1a, w1b, w2a, w2b,
    halo_ss, halo_rs, ss1, rs1, ss2, rs2,
):
    row, col = lax.axis_index("row"), lax.axis_index("col")
    z, quarter = row // QUAD, lax.rem(row, QUAD)

    barrier = pltpu.get_barrier_semaphore()

    def greet(device):
        pl.semaphore_signal(barrier, inc=1, device_id=device, device_id_type=MESH)

    for dr, dc in NEIGHBOURS:
        greet((lax.rem(row + dr + 32, 32), lax.rem(col + dc + SIDE, SIDE)))

    def greet_plane(t, _):
        other = lax.rem(col + t, SIDE)
        for k in range(QUAD):

            @pl.when(jnp.logical_or(t > 0, quarter != k))
            def _():
                greet((z * QUAD + k, other))

        @pl.when(jnp.logical_or(col != z, t > 0))
        def _():
            greet((col * QUAD + quarter, other))

        return 0

    lax.fori_loop(0, SIDE, greet_plane, 0)
    waits = 8 + 31 + SIDE - jnp.where(col == z, 1, 0)

    loads = {}
    for at, (name, source, target) in enumerate(
        (
            ("x", x_hbm, x_ref), ("1a", k1a_hbm, k1a), ("b1a", b1a_hbm, b1a),
            ("1b", k1b_hbm, k1b), ("b1b", b1b_hbm, b1b), ("2a", k2a_hbm, k2a),
            ("b2a", b2a_hbm, b2a), ("2b", k2b_hbm, k2b), ("b2b", b2b_hbm, b2b),
        )
    ):
        loads[name] = pltpu.make_async_copy(source, target, load_sem.at[at])
        loads[name].start()

    loads["x"].wait()

    def widen(g, _):
        flat[pl.ds(g * 512, 512), :] = x_ref[pl.ds(g * 16, 16)].astype(F32).reshape(512, 128)
        return 0

    lax.fori_loop(0, CHAN // 16, widen, 0)
    same = lax.broadcasted_iota(jnp.int32, (COLS, COLS), 0) == lax.broadcasted_iota(
        jnp.int32, (COLS, COLS), 1
    )
    unit = same.astype(F32).astype(BF16)

    def turn(t, _):
        for u in range(8):
            i = t * 8 + u
            line = flat[pl.ds(i, CHAN, stride=ROWS), :].astype(BF16)
            both = jnp.concatenate([line, line], axis=0)
            frame[ROW_PAD + i, COL_PAD : COL_PAD + COLS, :] = lax.dot_general(
                unit, both, NT, preferred_element_type=F32
            )
        return 0

    lax.fori_loop(0, ROWS // 8, turn, 0)

    def prepare_one():
        for name in ("1a", "b1a", "1b", "b1b"):
            loads[name].wait()
        for ky in range(3):
            for target, kernel in ((w1a, k1a), (w1b, k1b)):
                taps = three_taps(kernel, ky)
                target[:, ky * 256 : ky * 256 + 256] = jnp.concatenate([taps, taps], axis=0)

    def prepare_two():
        for name in ("2a", "b2a", "2b", "b2b"):
            loads[name].wait()
        zeros = jnp.zeros((CHAN, CHAN), BF16)
        for ky in range(3):
            w2a[:, ky * 256 : ky * 256 + 256] = jnp.concatenate(
                [three_taps(k2a, ky), three_taps(k2a, ky, True)], axis=0
            )
            for kx in range(3):
                upper = jnp.concatenate([k2b[ky, kx], zeros], axis=1)
                lower = jnp.concatenate([zeros, k2b[kx, ky]], axis=1)
                at = ky * 384 + kx * 128
                w2b[:, at : at + 128] = jnp.concatenate([upper, lower], axis=0)

    def bias(ref):
        return jnp.concatenate([ref[...], ref[...]], axis=1)

    def clear_outside():
        @pl.when(row == 0)
        def _():
            hidden[0:HID_ROW] = jnp.zeros((HID_ROW, 144, 128), F32)

        @pl.when(row == 31)
        def _():
            hidden[HID_ROW + ROWS :] = jnp.zeros((HID_ROW, 144, 128), F32)

        @pl.when(col == 0)
        def _():
            hidden[:, 0:HID_COL, :] = jnp.zeros((ROWS + 2 * HID_ROW, HID_COL, 128), F32)

        @pl.when(col == SIDE - 1)
        def _():
            hidden[:, HID_COL + COLS :, :] = jnp.zeros((ROWS + 2 * HID_ROW, HID_COL, 128), F32)

    halo = Halo(4, frame, halo_send.at[0], halo_recv.at[0], halo_ss.at[0], halo_rs.at[0], row, col)
    halo.pack()
    pl.semaphore_wait(barrier, waits)
    halo.start()
    prepare_one()
    halo.finish(SIDEWAYS)

    def shifted(d, top):
        def one(t, _):
            at = COL_PAD - HID_COL
            for u in range(4):
                i = top + t * 4 + u
                left = frame[i, at - d : at - d + 144, :]
                here = frame[i, at : at + 144, :]
                right = frame[i, at + d : at + d + 144, :]
                slab[i, :, 0:128] = paired(left, here).astype(BF16)
                slab[i, :, 128:256] = right.astype(BF16)
            return 0

        return one

    def conv_a(d, weights, bias_ref, first, step):
        def one(t, _):
            i = first + t * step
            lhs = jnp.concatenate(
                [
                    slab[pl.ds(i + ROW_PAD + (ky - 1) * d, step)].reshape(step * 144, 256)
                    for ky in range(3)
                ],
                axis=1,
            )
            total = lax.dot_general(lhs, weights[...], NT, preferred_element_type=F32)
            value = rounded(elu(total + bias(bias_ref)))
            hidden[pl.ds(i + HID_ROW, step)] = value.reshape(step, 144, 128)
            return 0

        return one

    lax.fori_loop(0, 8, shifted(2, ROW_PAD), 0)
    lax.fori_loop(0, 2, conv_a(2, w1a, b1a, 2, 14), 0)
    halo.finish(OTHERS)
    lax.fori_loop(0, 1, shifted(2, ROW_PAD - 4), 0)
    lax.fori_loop(0, 1, shifted(2, ROW_PAD + 32), 0)
    lax.fori_loop(0, 1, conv_a(2, w1a, b1a, -2, 4), 0)
    lax.fori_loop(0, 1, conv_a(2, w1a, b1a, 30, 4), 0)
    clear_outside()

    def hidden_taps(t, _):
        for u in range(4):
            i = t * 4 + u
            at = i + HID_ROW - 2
            left = hidden[at, HID_COL - 2 : HID_COL + 126, :]
            here = hidden[at, HID_COL : HID_COL + 128, :]
            right = hidden[at, HID_COL + 2 : HID_COL + 130, :]
            slab[i, 0:128, 0:128] = paired(left, here).astype(BF16)
            slab[i, 0:128, 128:256] = right.astype(BF16)
        return 0

    lax.fori_loop(0, 9, hidden_taps, 0)

    def conv_b_one(t, _):
        i = t * 16
        lhs = jnp.concatenate(
            [slab[pl.ds(i + 2 * ky, 16), 0:128, :].reshape(2048, 256) for ky in range(3)], axis=1
        )
        total = lax.dot_general(lhs, w1b[...], NT, preferred_element_type=F32)
        here = frame[pl.ds(ROW_PAD + i, 16), COL_PAD : COL_PAD + COLS, :].reshape(2048, 128)
        block_y[pl.ds(i * COLS, 2048), :] = rounded(elu(here + total + bias(b1b)))
        return 0

    lax.fori_loop(0, ROWS // 16, conv_b_one, 0)

    def spread(t, _):
        via = nearby(col, t)
        for k in range(QUAD):
            for u in range(4):
                column = block_y[pl.ds(32 * k + 4 * via + u, ROWS, stride=COLS), :]
                outbox[via, k, u] = paired(column[:16], column[16:]).astype(BF16)
            alone = jnp.logical_and(t == 0, quarter == k)

            @pl.when(alone)
            def _():
                pltpu.make_async_copy(
                    outbox.at[via, k], transit.at[col, quarter], rs1.at[col]
                ).start()

            @pl.when(jnp.logical_not(alone))
            def _():
                pltpu.make_async_remote_copy(
                    outbox.at[via, k],
                    transit.at[col, quarter],
                    ss1,
                    rs1.at[col],
                    device_id=(z * QUAD + k, via),
                    device_id_type=MESH,
                ).start()

        return 0

    lax.fori_loop(0, SIDE, spread, 0)

    def forward(t, _):
        origin = nearby(col, t)
        pltpu.make_async_copy(transit.at[origin], transit.at[origin], rs1.at[origin]).wait()
        alone = jnp.logical_and(origin == z, col == z)

        @pl.when(alone)
        def _():
            pltpu.make_async_copy(transit.at[origin], inbox.at[col], rs2.at[col]).start()

        @pl.when(jnp.logical_not(alone))
        def _():
            pltpu.make_async_remote_copy(
                transit.at[origin],
                inbox.at[col],
                ss2,
                rs2.at[col],
                device_id=(origin * QUAD + quarter, z),
                device_id_type=MESH,
            ).start()

        return 0

    lax.fori_loop(0, SIDE, forward, 0)
    prepare_two()

    def arrive(t, _):
        via = nearby(z, t)
        pltpu.make_async_copy(inbox.at[via], inbox.at[via], rs2.at[via]).wait()
        for u in range(4):
            i = via * 4 + u
            for k in range(QUAD):
                mirror = doubled(inbox[via, k, u].astype(F32))
                for half in range(2):
                    j = 32 * k + 16 * half
                    own = block_y[pl.ds(pl.multiple_of(i * COLS + j, 16), 16), :]
                    frame[ROW_PAD + i, COL_PAD + j : COL_PAD + j + 16, :] = rounded(
                        (own + mirror[half]) * 0.5
                    )
        return 0

    lax.fori_loop(0, SIDE, arrive, 0)

    halo = Halo(8, frame, halo_send.at[1], halo_recv.at[1], halo_ss.at[1], halo_rs.at[1], row, col)
    halo.pack(True)
    halo.finish(SIDEWAYS)

    lax.fori_loop(0, 8, shifted(4, ROW_PAD), 0)
    lax.fori_loop(0, 2, conv_a(4, w2a, b2a, 4, 12), 0)
    halo.finish(OTHERS)
    lax.fori_loop(0, 2, shifted(4, 0), 0)
    lax.fori_loop(0, 2, shifted(4, ROW_PAD + 32), 0)
    lax.fori_loop(0, 1, conv_a(4, w2a, b2a, -4, 8), 0)
    lax.fori_loop(0, 1, conv_a(4, w2a, b2a, 28, 8), 0)
    clear_outside()

    def wide_taps(t, _):
        for u in range(4):
            i = t * 4 + u
            for kx in range(3):
                at = HID_COL + 4 * (kx - 1)
                wide[i, :, kx * 128 : kx * 128 + 128] = hidden[i, at : at + 128, :].astype(BF16)
        return 0

    lax.fori_loop(0, 10, wide_taps, 0)

    lane = lax.broadcasted_iota(jnp.int32, (CHAN, 128), 1)
    chan = lax.broadcasted_iota(jnp.int32, (CHAN, 128), 0)
    mean = jnp.where(jnp.logical_or(lane == chan, lane == chan + CHAN), 0.5, 0.0).astype(BF16)

    def conv_b_two(t, _):
        i = t * 8
        lhs = jnp.concatenate(
            [wide[pl.ds(i + 4 * ky, 8)].reshape(1024, 384) for ky in range(3)], axis=1
        )
        total = lax.dot_general(lhs, w2b[...], NT, preferred_element_type=F32)
        here = frame[pl.ds(ROW_PAD + i, 8), COL_PAD : COL_PAD + COLS, :].reshape(1024, 128)
        both = elu(here + total + bias(b2b)).astype(BF16)
        for u in range(8):
            line = both[u * COLS : (u + 1) * COLS]
            flat[pl.ds(i + u, CHAN, stride=ROWS), :] = lax.dot_general(
                mean, line, NT, preferred_element_type=F32
            )
        return 0

    lax.fori_loop(0, ROWS // 8, conv_b_two, 0)

    def narrow(g, _):
        out_ref[pl.ds(g * 8, 8)] = flat[pl.ds(g * 256, 256), :].reshape(8, ROWS, COLS).astype(BF16)
        return 0

    lax.fori_loop(0, CHAN // 8, narrow, 0)

    def sent_one(t, _):
        for k in range(QUAD):

            @pl.when(jnp.logical_not(jnp.logical_and(t == 0, quarter == k)))
            def _():
                pltpu.make_async_copy(outbox.at[0, 0], outbox.at[0, 0], ss1).wait()

        @pl.when(jnp.logical_or(t > 0, col != z))
        def _():
            pltpu.make_async_copy(transit.at[0], transit.at[0], ss2).wait()

        return 0

    lax.fori_loop(0, SIDE, sent_one, 0)


def shards(pair_map, k1a, b1a, k1b, b1b, k2a, b2a, k2b, b2b):
    wide = lambda b: b.reshape(1, CHAN)
    vmem = pl.BlockSpec(memory_space=pltpu.VMEM)
    dma, regular = pltpu.SemaphoreType.DMA, pltpu.SemaphoreType.REGULAR
    return pl.pallas_call(
        body,
        out_shape=jax.ShapeDtypeStruct((CHAN, ROWS, COLS), BF16),
        in_specs=[pl.BlockSpec(memory_space=pl.ANY)] * 9,
        out_specs=vmem,
        scratch_shapes=[
            pltpu.VMEM((CHAN, ROWS, COLS), BF16),
            *[pltpu.VMEM((3, 3, CHAN, CHAN), BF16) for _ in range(4)],
            *[pltpu.VMEM((1, CHAN), F32) for _ in range(4)],
            dma((9,)),
            pltpu.VMEM((CHAN * ROWS, COLS), F32),
            pltpu.VMEM((ROWS + 2 * ROW_PAD, COLS + 2 * COL_PAD, 128), F32),
            pltpu.VMEM((ROWS + 2 * ROW_PAD, 144, 256), BF16),
            pltpu.VMEM((ROWS + 2 * HID_ROW, 144, 128), F32),
            pltpu.VMEM((ROWS + 2 * HID_ROW, COLS, 384), BF16),
            pltpu.VMEM((ROWS * COLS, 128), F32),
            pltpu.VMEM((SIDE, QUAD, 4, 16, 128), BF16),
            pltpu.VMEM((SIDE, QUAD, 4, 16, 128), BF16),
            pltpu.VMEM((SIDE, QUAD, 4, 16, 128), BF16),
            pltpu.VMEM((2, 8, 32, 16, 128), BF16),
            pltpu.VMEM((2, 8, 32, 16, 128), BF16),
            pltpu.VMEM((128, 768), BF16),
            pltpu.VMEM((128, 768), BF16),
            pltpu.VMEM((128, 768), BF16),
            pltpu.VMEM((128, 1152), BF16),
            dma((2, 8)),
            dma((2, 8)),
            dma,
            dma((SIDE,)),
            dma,
            dma((SIDE,)),
        ],
        compiler_params=pltpu.CompilerParams(
            collective_id=0, has_side_effects=True, vmem_limit_bytes=50 << 20
        ),
    )(pair_map, k1a, wide(b1a), k1b, wide(b1b), k2a, wide(b2a), k2b, wide(b2b))


def solution(mesh):
    placed = (P(None, "row", "col"), P(), P(), P(), P(), P(), P(), P(), P())
    return jax.shard_map(
        shards, mesh=mesh, in_specs=placed, out_specs=P(None, "row", "col"), check_vma=False
    )
```

profile of v0, /device:TPU:1, one launch (start us, length us, event | category | flops | bytes accessed | tf_op | source)
XLA Modules:
  0.0 66.5 jit_solution(16216127524065946680)
XLA Ops:
  0.0 0.0 copy-start.8
  0.0 0.0 copy-start.5
  0.0 0.0 copy-start.6
  0.0 0.0 copy-start.7
  0.0 0.6 copy-done.8
  0.7 0.0 copy-done.5
  0.7 0.0 copy-done.6
  0.7 0.0 copy-done.7
  0.7 0.0 copy-start
  0.7 1.0 %copy-done = bf16[64,32,128]{2,1,0:T(8,128)(2,1)S(1)} copy-done((bf16[64,32,128]{2,1,0:T(8,128)(2,1)S(1)}, bf16[64,32,128]{2,1,0:T(8,128)(2,1)}, u32[]{:S(2)}) %copy-start) | copy-done | bytes 524312
  1.7 0.0 copy-start.1
  1.7 0.9 %copy-done.1 = bf16[3,3,64,64]{3,2,1,0:T(8,128)(2,1)S(1)} copy-done((bf16[3,3,64,64]{3,2,1,0:T(8,128)(2,1)S(1)}, bf16[3,3,64,64]{3,2,1,0:T(8,128)(2,1)}, u32[]{:S(2)}) %copy-start.1) | copy-done | bytes 73752
  2.7 0.0 copy-start.2
  2.7 0.9 %copy-done.2 = bf16[3,3,64,64]{3,2,1,0:T(8,128)(2,1)S(1)} copy-done((bf16[3,3,64,64]{3,2,1,0:T(8,128)(2,1)S(1)}, bf16[3,3,64,64]{3,2,1,0:T(8,128)(2,1)}, u32[]{:S(2)}) %copy-start.2) | copy-done | bytes 73752
  3.6 0.0 copy-start.3
  3.6 0.9 %copy-done.3 = bf16[3,3,64,64]{3,2,1,0:T(8,128)(2,1)S(1)} copy-done((bf16[3,3,64,64]{3,2,1,0:T(8,128)(2,1)S(1)}, bf16[3,3,64,64]{3,2,1,0:T(8,128)(2,1)}, u32[]{:S(2)}) %copy-start.3) | copy-done | bytes 73752
  4.5 0.0 copy-start.4
  4.5 0.9 %copy-done.4 = bf16[3,3,64,64]{3,2,1,0:T(8,128)(2,1)S(1)} copy-done((bf16[3,3,64,64]{3,2,1,0:T(8,128)(2,1)S(1)}, bf16[3,3,64,64]{3,2,1,0:T(8,128)(2,1)}, u32[]{:S(2)}) %copy-start.4) | copy-done | bytes 73752
  5.4 60.3 %shard_map.91 = bf16[64,32,128]{2,1,0:T(8,128)(2,1)S(1)} custom-call(bf16[64,32,128]{2,1,0:T(8,128)(2,1)S(1)} %copy-done, bf16[3,3,64,64]{3,2,1,0:T(8,128)(2,1)S(1)} %copy-done.1, f32[1,64]{1,0:T(1,128)S(1)} %bitcast.4, bf16[3,3,64,64]{3,2,1,0:T(8,128)(2,1)S(1)} %copy-done.2, f32[1,64]{1,0:T(1,128)S(1)} %bitcast.5, bf16[3,3,64,64]{3,2,1,0:T(8,128)(2,1)S(1)} %copy-done.3, ...), custom_call_target="tpu_custom_call" | custom-call | tf_op jit(solution)/shard_map/pallas_call | solution.py:475
  65.7 0.8 %copy.11 = bf16[64,32,128]{2,1,0:T(8,128)(2,1)} copy(bf16[64,32,128]{2,1,0:T(8,128)(2,1)S(1)} %shard_map.91) | data formatting | bytes 1048576
Async XLA Ops:
  0.0 0.7 copy-start.8
  0.0 0.7 %copy-start.5 = (f32[64]{0:T(128)S(1)}, f32[64]{0:T(128)}, u32[]{:S(2)}) copy-start(f32[64]{0:T(128)} %param.11) | copy-start | bytes 772
  0.0 0.7 %copy-start.6 = (f32[64]{0:T(128)S(1)}, f32[64]{0:T(128)}, u32[]{:S(2)}) copy-start(f32[64]{0:T(128)} %param.13) | copy-start | bytes 772
  0.0 0.7 %copy-start.7 = (f32[64]{0:T(128)S(1)}, f32[64]{0:T(128)}, u32[]{:S(2)}) copy-start(f32[64]{0:T(128)} %param.15) | copy-start | bytes 772
  0.7 1.0 %copy-start = (bf16[64,32,128]{2,1,0:T(8,128)(2,1)S(1)}, bf16[64,32,128]{2,1,0:T(8,128)(2,1)}, u32[]{:S(2)}) copy-start(bf16[64,32,128]{2,1,0:T(8,128)(2,1)} %x_hbm.1) | copy-start | bytes 1572868
  1.7 0.9 %copy-start.1 = (bf16[3,3,64,64]{3,2,1,0:T(8,128)(2,1)S(1)}, bf16[3,3,64,64]{3,2,1,0:T(8,128)(2,1)}, u32[]{:S(2)}) copy-start(bf16[3,3,64,64]{3,2,1,0:T(8,128)(2,1)} %k1a_hbm.1) | copy-start | bytes 221188
  2.7 0.9 %copy-start.2 = (bf16[3,3,64,64]{3,2,1,0:T(8,128)(2,1)S(1)}, bf16[3,3,64,64]{3,2,1,0:T(8,128)(2,1)}, u32[]{:S(2)}) copy-start(bf16[3,3,64,64]{3,2,1,0:T(8,128)(2,1)} %k1b_hbm.1) | copy-start | bytes 221188
  3.6 0.9 %copy-start.3 = (bf16[3,3,64,64]{3,2,1,0:T(8,128)(2,1)S(1)}, bf16[3,3,64,64]{3,2,1,0:T(8,128)(2,1)}, u32[]{:S(2)}) copy-start(bf16[3,3,64,64]{3,2,1,0:T(8,128)(2,1)} %k2a_hbm.1) | copy-start | bytes 221188
  4.5 0.9 %copy-start.4 = (bf16[3,3,64,64]{3,2,1,0:T(8,128)(2,1)S(1)}, bf16[3,3,64,64]{3,2,1,0:T(8,128)(2,1)}, u32[]{:S(2)}) copy-start(bf16[3,3,64,64]{3,2,1,0:T(8,128)(2,1)} %k2b_hbm.1) | copy-start | bytes 221188
where the time goes:
time: 66.7 us; the launch traced here: 66.5 us
  Pallas kernels  60.3 us (90%)
  local copies, waits for them, and re-layouts  6.16 us (9%)
    pallas_call x1, Pallas kernels, shards(): pl.pallas_call(body, out_shape=jax.ShapeDtypeStruct((CHAN, ROWS, COLS), B...  60.3 us
    unnamed x19, local copies, waits for them, and re-layouts  6.16 us

commit v1 on v0

--- a/solution.py
+++ b/solution.py
@@ -47,6 +47,10 @@
         + lax.rem(at // 2 + middle, 2) * 2
         + lax.rem(at + step, 2)
     )
+
+
+def rows_at(step):
+    return 2 * lax.rem(3 * (step // 2), 4) + lax.rem(step, 2)
 
 
 class Halo:
@@ -84,9 +88,9 @@
         there = self.recv.at[mine, pl.ds(0, count)]
         return pltpu.make_async_copy(there, there, self.recv_sem.at[mine])
 
-    def pack(self, start=False):
+    def pack(self, which, start=False):
         frame, rows = self.frame, self.rows
-        for at in ORDER:
+        for at in which:
             dr, dc = NEIGHBOURS[at]
             mine, _ = self.parts(at)
             top = ROW_PAD if dr < 0 else ROW_PAD + ROWS - rows
@@ -260,45 +264,54 @@
             hidden[:, HID_COL + COLS :, :] = jnp.zeros((ROWS + 2 * HID_ROW, HID_COL, 128), F32)
 
     halo = Halo(4, frame, halo_send.at[0], halo_recv.at[0], halo_ss.at[0], halo_rs.at[0], row, col)
-    halo.pack()
+    halo.pack(ORDER)
     pl.semaphore_wait(barrier, waits)
     halo.start()
     prepare_one()
-    halo.finish(SIDEWAYS)
-
-    def shifted(d, top):
+
+    everywhere, borders = ((0, 144),), ((0, 16), (128, 144))
+
+    def shifted(d, top, spans=everywhere):
         def one(t, _):
-            at = COL_PAD - HID_COL
             for u in range(4):
                 i = top + t * 4 + u
-                left = frame[i, at - d : at - d + 144, :]
-                here = frame[i, at : at + 144, :]
-                right = frame[i, at + d : at + d + 144, :]
-                slab[i, :, 0:128] = paired(left, here).astype(BF16)
-                slab[i, :, 128:256] = right.astype(BF16)
+                for low, high in spans:
+                    at, many = COL_PAD - HID_COL + low, high - low
+                    left = frame[i, at - d : at - d + many, :]
+                    here = frame[i, at : at + many, :]
+                    right = frame[i, at + d : at + d + many, :]
+                    slab[i, low:high, 0:128] = paired(left, here).astype(BF16)
+                    slab[i, low:high, 128:256] = right.astype(BF16)
             return 0
 
         return one
 
-    def conv_a(d, weights, bias_ref, first, step):
+    def conv_a(d, weights, bias_ref, first, step, spans=everywhere):
         def one(t, _):
             i = first + t * step
-            lhs = jnp.concatenate(
-                [
-                    slab[pl.ds(i + ROW_PAD + (ky - 1) * d, step)].reshape(step * 144, 256)
-                    for ky in range(3)
-                ],
-                axis=1,
-            )
-            total = lax.dot_general(lhs, weights[...], NT, preferred_element_type=F32)
-            value = rounded(elu(total + bias(bias_ref)))
-            hidden[pl.ds(i + HID_ROW, step)] = value.reshape(step, 144, 128)
+            for low, high in spans:
+                many = high - low
+                lhs = jnp.concatenate(
+                    [
+                        slab[pl.ds(i + ROW_PAD + ky * d, step), low:high, :].reshape(
+                            step * many, 256
+                        )
+                        for ky in (-1, 0, 1)
+                    ],
+                    axis=1,
+                )
+                total = lax.dot_general(lhs, weights[...], NT, preferred_element_type=F32)
+                value = rounded(elu(total + bias(bias_ref)))
+                hidden[pl.ds(i + HID_ROW, step), low:high, :] = value.reshape(step, many, 128)
             return 0
 
         return one
 
     lax.fori_loop(0, 8, shifted(2, ROW_PAD), 0)
     lax.fori_loop(0, 2, conv_a(2, w1a, b1a, 2, 14), 0)
+    halo.finish(SIDEWAYS)
+    lax.fori_loop(0, 8, shifted(2, ROW_PAD, borders), 0)
+    lax.fori_loop(0, 1, conv_a(2, w1a, b1a, 2, 28, borders), 0)
     halo.finish(OTHERS)
     lax.fori_loop(0, 1, shifted(2, ROW_PAD - 4), 0)
     lax.fori_loop(0, 1, shifted(2, ROW_PAD + 32), 0)
@@ -335,7 +348,7 @@
         via = nearby(col, t)
         for k in range(QUAD):
             for u in range(4):
-                column = block_y[pl.ds(32 * k + 4 * via + u, ROWS, stride=COLS), :]
+                column = block_y[pl.ds(32 * k + 4 * rows_at(t) + u, ROWS, stride=COLS), :]
                 outbox[via, k, u] = paired(column[:16], column[16:]).astype(BF16)
             alone = jnp.logical_and(t == 0, quarter == k)
 
@@ -389,7 +402,7 @@
         via = nearby(z, t)
         pltpu.make_async_copy(inbox.at[via], inbox.at[via], rs2.at[via]).wait()
         for u in range(4):
-            i = via * 4 + u
+            i = rows_at(t) * 4 + u
             for k in range(QUAD):
                 mirror = doubled(inbox[via, k, u].astype(F32))
                 for half in range(2):
@@ -400,19 +413,18 @@
                     )
         return 0
 
-    lax.fori_loop(0, SIDE, arrive, 0)
-
     halo = Halo(8, frame, halo_send.at[1], halo_recv.at[1], halo_ss.at[1], halo_rs.at[1], row, col)
-    halo.pack(True)
+    lax.fori_loop(0, SIDE // 2, arrive, 0)
+    halo.pack(OTHERS, True)
+    lax.fori_loop(SIDE // 2, SIDE, arrive, 0)
+    halo.pack(SIDEWAYS, True)
+    halo.finish(OTHERS)
+
+    lax.fori_loop(0, 12, shifted(4, 0), 0)
+    lax.fori_loop(0, 2, conv_a(4, w2a, b2a, -4, 20), 0)
     halo.finish(SIDEWAYS)
-
-    lax.fori_loop(0, 8, shifted(4, ROW_PAD), 0)
-    lax.fori_loop(0, 2, conv_a(4, w2a, b2a, 4, 12), 0)
-    halo.finish(OTHERS)
-    lax.fori_loop(0, 2, shifted(4, 0), 0)
-    lax.fori_loop(0, 2, shifted(4, ROW_PAD + 32), 0)
-    lax.fori_loop(0, 1, conv_a(4, w2a, b2a, -4, 8), 0)
-    lax.fori_loop(0, 1, conv_a(4, w2a, b2a, 28, 8), 0)
+    lax.fori_loop(0, 12, shifted(4, 0, borders), 0)
+    lax.fori_loop(0, 1, conv_a(4, w2a, b2a, -4, 40, borders), 0)
     clear_outside()
 
     def wide_taps(t, _):

time: 66.7 us -> 62.3 us (0.934)
  Pallas kernels: 60.3 us -> 55.6 us
    pallas_call x1, Pallas kernels: 60.3 us -> 55.6 us  [shards(): pl.pallas_call(body, out_shape=jax.ShapeDtypeStruct((CHAN, ROWS, COLS), B...]
where the time goes in v1:
time: 62.3 us; the launch traced here: 61.8 us
  Pallas kernels  55.6 us (89%)
  local copies, waits for them, and re-layouts  6.16 us (10%)
    pallas_call x1, Pallas kernels, shards(): pl.pallas_call(body, out_shape=jax.ShapeDtypeStruct((CHAN, ROWS, COLS), B...  55.6 us
    unnamed x19, local copies, waits for them, and re-layouts  6.16 us

profile of v1, /device:TPU:1, one launch (start us, length us, event | category | flops | bytes accessed | tf_op | source)
XLA Modules:
  0.0 61.8 jit_solution(16637348397255199804)
XLA Ops:
  0.0 0.0 copy-start.8
  0.0 0.0 copy-start.5
  0.0 0.0 copy-start.6
  0.0 0.0 copy-start.7
  0.0 0.6 %copy-done.8 = f32[64]{0:T(128)S(1)} copy-done((f32[64]{0:T(128)S(1)}, f32[64]{0:T(128)}, u32[]{:S(2)}) %copy-start.8) | copy-done | bytes 280
  0.7 0.0 copy-done.5
  0.7 0.0 copy-done.6
  0.7 0.0 copy-done.7
  0.7 0.0 copy-start
  0.7 1.0 %copy-done = bf16[64,32,128]{2,1,0:T(8,128)(2,1)S(1)} copy-done((bf16[64,32,128]{2,1,0:T(8,128)(2,1)S(1)}, bf16[64,32,128]{2,1,0:T(8,128)(2,1)}, u32[]{:S(2)}) %copy-start) | copy-done | bytes 524312
  1.7 0.0 copy-start.1
  1.7 0.9 %copy-done.1 = bf16[3,3,64,64]{3,2,1,0:T(8,128)(2,1)S(1)} copy-done((bf16[3,3,64,64]{3,2,1,0:T(8,128)(2,1)S(1)}, bf16[3,3,64,64]{3,2,1,0:T(8,128)(2,1)}, u32[]{:S(2)}) %copy-start.1) | copy-done | bytes 73752
  2.7 0.0 copy-start.2
  2.7 0.9 %copy-done.2 = bf16[3,3,64,64]{3,2,1,0:T(8,128)(2,1)S(1)} copy-done((bf16[3,3,64,64]{3,2,1,0:T(8,128)(2,1)S(1)}, bf16[3,3,64,64]{3,2,1,0:T(8,128)(2,1)}, u32[]{:S(2)}) %copy-start.2) | copy-done | bytes 73752
  3.6 0.0 copy-start.3
  3.6 0.9 %copy-done.3 = bf16[3,3,64,64]{3,2,1,0:T(8,128)(2,1)S(1)} copy-done((bf16[3,3,64,64]{3,2,1,0:T(8,128)(2,1)S(1)}, bf16[3,3,64,64]{3,2,1,0:T(8,128)(2,1)}, u32[]{:S(2)}) %copy-start.3) | copy-done | bytes 73752
  4.5 0.0 copy-start.4
  4.5 0.9 %copy-done.4 = bf16[3,3,64,64]{3,2,1,0:T(8,128)(2,1)S(1)} copy-done((bf16[3,3,64,64]{3,2,1,0:T(8,128)(2,1)S(1)}, bf16[3,3,64,64]{3,2,1,0:T(8,128)(2,1)}, u32[]{:S(2)}) %copy-start.4) | copy-done | bytes 73752
  5.4 55.6 %shard_map.91 = bf16[64,32,128]{2,1,0:T(8,128)(2,1)S(1)} custom-call(bf16[64,32,128]{2,1,0:T(8,128)(2,1)S(1)} %copy-done, bf16[3,3,64,64]{3,2,1,0:T(8,128)(2,1)S(1)} %copy-done.1, f32[1,64]{1,0:T(1,128)S(1)} %bitcast.4, bf16[3,3,64,64]{3,2,1,0:T(8,128)(2,1)S(1)} %copy-done.2, f32[1,64]{1,0:T(1,128)S(1)} %bitcast.5, bf16[3,3,64,64]{3,2,1,0:T(8,128)(2,1)S(1)} %copy-done.3, ...), custom_call_target="tpu_custom_call" | custom-call | tf_op jit(solution)/shard_map/pallas_call | solution.py:487
  61.0 0.8 %copy.11 = bf16[64,32,128]{2,1,0:T(8,128)(2,1)} copy(bf16[64,32,128]{2,1,0:T(8,128)(2,1)S(1)} %shard_map.91) | data formatting | bytes 1048576
Async XLA Ops:
  0.0 0.7 %copy-start.8 = (f32[64]{0:T(128)S(1)}, f32[64]{0:T(128)}, u32[]{:S(2)}) copy-start(f32[64]{0:T(128)} %param.17) | copy-start | bytes 772
  0.0 0.7 %copy-start.5 = (f32[64]{0:T(128)S(1)}, f32[64]{0:T(128)}, u32[]{:S(2)}) copy-start(f32[64]{0:T(128)} %param.11) | copy-start | bytes 772
  0.0 0.7 %copy-start.6 = (f32[64]{0:T(128)S(1)}, f32[64]{0:T(128)}, u32[]{:S(2)}) copy-start(f32[64]{0:T(128)} %param.13) | copy-start | bytes 772
  0.0 0.7 %copy-start.7 = (f32[64]{0:T(128)S(1)}, f32[64]{0:T(128)}, u32[]{:S(2)}) copy-start(f32[64]{0:T(128)} %param.15) | copy-start | bytes 772
  0.7 1.0 %copy-start = (bf16[64,32,128]{2,1,0:T(8,128)(2,1)S(1)}, bf16[64,32,128]{2,1,0:T(8,128)(2,1)}, u32[]{:S(2)}) copy-start(bf16[64,32,128]{2,1,0:T(8,128)(2,1)} %x_hbm.1) | copy-start | bytes 1572868
  1.7 0.9 %copy-start.1 = (bf16[3,3,64,64]{3,2,1,0:T(8,128)(2,1)S(1)}, bf16[3,3,64,64]{3,2,1,0:T(8,128)(2,1)}, u32[]{:S(2)}) copy-start(bf16[3,3,64,64]{3,2,1,0:T(8,128)(2,1)} %k1a_hbm.1) | copy-start | bytes 221188
  2.7 0.9 %copy-start.2 = (bf16[3,3,64,64]{3,2,1,0:T(8,128)(2,1)S(1)}, bf16[3,3,64,64]{3,2,1,0:T(8,128)(2,1)}, u32[]{:S(2)}) copy-start(bf16[3,3,64,64]{3,2,1,0:T(8,128)(2,1)} %k1b_hbm.1) | copy-start | bytes 221188
  3.6 0.9 %copy-start.3 = (bf16[3,3,64,64]{3,2,1,0:T(8,128)(2,1)S(1)}, bf16[3,3,64,64]{3,2,1,0:T(8,128)(2,1)}, u32[]{:S(2)}) copy-start(bf16[3,3,64,64]{3,2,1,0:T(8,128)(2,1)} %k2a_hbm.1) | copy-start | bytes 221188
  4.5 0.9 %copy-start.4 = (bf16[3,3,64,64]{3,2,1,0:T(8,128)(2,1)S(1)}, bf16[3,3,64,64]{3,2,1,0:T(8,128)(2,1)}, u32[]{:S(2)}) copy-start(bf16[3,3,64,64]{3,2,1,0:T(8,128)(2,1)} %k2b_hbm.1) | copy-start | bytes 221188

commit v2 on v1

--- a/solution.py
+++ b/solution.py
@@ -161,6 +161,9 @@
     row, col = lax.axis_index("row"), lax.axis_index("col")
     z, quarter = row // QUAD, lax.rem(row, QUAD)
 
+    loads = {"x": pltpu.make_async_copy(x_hbm, x_ref, load_sem.at[0])}
+    loads["x"].start()
+
     barrier = pltpu.get_barrier_semaphore()
 
     def greet(device):
@@ -186,15 +189,14 @@
     lax.fori_loop(0, SIDE, greet_plane, 0)
     waits = 8 + 31 + SIDE - jnp.where(col == z, 1, 0)
 
-    loads = {}
     for at, (name, source, target) in enumerate(
         (
-            ("x", x_hbm, x_ref), ("1a", k1a_hbm, k1a), ("b1a", b1a_hbm, b1a),
+            ("1a", k1a_hbm, k1a), ("b1a", b1a_hbm, b1a),
             ("1b", k1b_hbm, k1b), ("b1b", b1b_hbm, b1b), ("2a", k2a_hbm, k2a),
             ("b2a", b2a_hbm, b2a), ("2b", k2b_hbm, k2b), ("b2b", b2b_hbm, b2b),
         )
     ):
-        loads[name] = pltpu.make_async_copy(source, target, load_sem.at[at])
+        loads[name] = pltpu.make_async_copy(source, target, load_sem.at[at + 1])
         loads[name].start()
 
     loads["x"].wait()
@@ -307,8 +309,49 @@
 
         return one
 
+    full, sides = ((0, 128),), ((0, 16), (112, 128))
+
+    def hidden_taps(first, spans):
+        def one(t, _):
+            for u in range(4):
+                i = first + t * 4 + u
+                at = i + HID_ROW
+                for low, high in spans:
+                    left = hidden[at, HID_COL - 2 + low : HID_COL - 2 + high, :]
+                    here = hidden[at, HID_COL + low : HID_COL + high, :]
+                    right = hidden[at, HID_COL + 2 + low : HID_COL + 2 + high, :]
+                    wide[i + 2, low:high, 0:128] = paired(left, here).astype(BF16)
+                    wide[i + 2, low:high, 128:256] = right.astype(BF16)
+            return 0
+
+        return one
+
+    def conv_b_one(first, step, spans):
+        def one(t, _):
+            i = first + t * step
+            for low, high in spans:
+                many = high - low
+                lhs = jnp.concatenate(
+                    [
+                        wide[pl.ds(i + 2 * ky, step), low:high, 0:256].reshape(step * many, 256)
+                        for ky in range(3)
+                    ],
+                    axis=1,
+                )
+                total = lax.dot_general(lhs, w1b[...], NT, preferred_element_type=F32)
+                here = frame[pl.ds(ROW_PAD + i, step), COL_PAD + low : COL_PAD + high, :]
+                value = rounded(elu(here.reshape(step * many, 128) + total + bias(b1b)))
+                for u in range(step):
+                    at = pl.multiple_of((i + u) * COLS + low, 16)
+                    block_y[pl.ds(at, many), :] = value[u * many : (u + 1) * many]
+            return 0
+
+        return one
+
     lax.fori_loop(0, 8, shifted(2, ROW_PAD), 0)
     lax.fori_loop(0, 2, conv_a(2, w1a, b1a, 2, 14), 0)
+    lax.fori_loop(0, 7, hidden_taps(2, full), 0)
+    lax.fori_loop(0, 2, conv_b_one(4, 12, full), 0)
     halo.finish(SIDEWAYS)
     lax.fori_loop(0, 8, shifted(2, ROW_PAD, borders), 0)
     lax.fori_loop(0, 1, conv_a(2, w1a, b1a, 2, 28, borders), 0)
@@ -318,31 +361,12 @@
     lax.fori_loop(0, 1, conv_a(2, w1a, b1a, -2, 4), 0)
     lax.fori_loop(0, 1, conv_a(2, w1a, b1a, 30, 4), 0)
     clear_outside()
-
-    def hidden_taps(t, _):
-        for u in range(4):
-            i = t * 4 + u
-            at = i + HID_ROW - 2
-            left = hidden[at, HID_COL - 2 : HID_COL + 126, :]
-            here = hidden[at, HID_COL : HID_COL + 128, :]
-            right = hidden[at, HID_COL + 2 : HID_COL + 130, :]
-            slab[i, 0:128, 0:128] = paired(left, here).astype(BF16)
-            slab[i, 0:128, 128:256] = right.astype(BF16)
-        return 0
-
-    lax.fori_loop(0, 9, hidden_taps, 0)
-
-    def conv_b_one(t, _):
-        i = t * 16
-        lhs = jnp.concatenate(
-            [slab[pl.ds(i + 2 * ky, 16), 0:128, :].reshape(2048, 256) for ky in range(3)], axis=1
-        )
-        total = lax.dot_general(lhs, w1b[...], NT, preferred_element_type=F32)
-        here = frame[pl.ds(ROW_PAD + i, 16), COL_PAD : COL_PAD + COLS, :].reshape(2048, 128)
-        block_y[pl.ds(i * COLS, 2048), :] = rounded(elu(here + total + bias(b1b)))
-        return 0
-
-    lax.fori_loop(0, ROWS // 16, conv_b_one, 0)
+    lax.fori_loop(0, 1, hidden_taps(-2, full), 0)
+    lax.fori_loop(0, 1, hidden_taps(30, full), 0)
+    lax.fori_loop(0, 7, hidden_taps(2, sides), 0)
+    lax.fori_loop(0, 1, conv_b_one(0, 4, full), 0)
+    lax.fori_loop(0, 1, conv_b_one(28, 4, full), 0)
+    lax.fori_loop(0, 1, conv_b_one(4, 24, sides), 0)
 
     def spread(t, _):
         via = nearby(col, t)

time: 62.3 us -> 61.6 us (0.989)
  Pallas kernels: 55.6 us -> 54.4 us
    pallas_call x1, Pallas kernels: 55.6 us -> 54.4 us  [shards(): pl.pallas_call(body, out_shape=jax.ShapeDtypeStruct((CHAN, ROWS, COLS), B...]
where the time goes in v2:
time: 61.6 us; the launch traced here: 60.6 us
  Pallas kernels  54.4 us (88%)
  local copies, waits for them, and re-layouts  6.16 us (10%)
    pallas_call x1, Pallas kernels, shards(): pl.pallas_call(body, out_shape=jax.ShapeDtypeStruct((CHAN, ROWS, COLS), B...  54.4 us
    unnamed x19, local copies, waits for them, and re-layouts  6.16 us

profile of v2, /device:TPU:1, one launch (start us, length us, event | category | flops | bytes accessed | tf_op | source)
XLA Modules:
  0.0 60.6 jit_solution(1759072664952977920)
XLA Ops:
  0.0 0.0 copy-start.8
  0.0 0.0 copy-start.5
  0.0 0.0 copy-start.6
  0.0 0.0 copy-start.7
  0.0 0.6 %copy-done.8 = f32[64]{0:T(128)S(1)} copy-done((f32[64]{0:T(128)S(1)}, f32[64]{0:T(128)}, u32[]{:S(2)}) %copy-start.8) | copy-done | bytes 280
  0.7 0.0 copy-done.5
  0.7 0.0 copy-done.6
  0.7 0.0 copy-done.7
  0.7 0.0 copy-start
  0.7 1.0 %copy-done = bf16[64,32,128]{2,1,0:T(8,128)(2,1)S(1)} copy-done((bf16[64,32,128]{2,1,0:T(8,128)(2,1)S(1)}, bf16[64,32,128]{2,1,0:T(8,128)(2,1)}, u32[]{:S(2)}) %copy-start) | copy-done | bytes 524312
  1.7 0.0 copy-start.1
  1.7 0.9 %copy-done.1 = bf16[3,3,64,64]{3,2,1,0:T(8,128)(2,1)S(1)} copy-done((bf16[3,3,64,64]{3,2,1,0:T(8,128)(2,1)S(1)}, bf16[3,3,64,64]{3,2,1,0:T(8,128)(2,1)}, u32[]{:S(2)}) %copy-start.1) | copy-done | bytes 73752
  2.7 0.0 copy-start.2
  2.7 0.9 %copy-done.2 = bf16[3,3,64,64]{3,2,1,0:T(8,128)(2,1)S(1)} copy-done((bf16[3,3,64,64]{3,2,1,0:T(8,128)(2,1)S(1)}, bf16[3,3,64,64]{3,2,1,0:T(8,128)(2,1)}, u32[]{:S(2)}) %copy-start.2) | copy-done | bytes 73752
  3.6 0.0 copy-start.3
  3.6 0.9 %copy-done.3 = bf16[3,3,64,64]{3,2,1,0:T(8,128)(2,1)S(1)} copy-done((bf16[3,3,64,64]{3,2,1,0:T(8,128)(2,1)S(1)}, bf16[3,3,64,64]{3,2,1,0:T(8,128)(2,1)}, u32[]{:S(2)}) %copy-start.3) | copy-done | bytes 73752
  4.5 0.0 copy-start.4
  4.5 0.9 %copy-done.4 = bf16[3,3,64,64]{3,2,1,0:T(8,128)(2,1)S(1)} copy-done((bf16[3,3,64,64]{3,2,1,0:T(8,128)(2,1)S(1)}, bf16[3,3,64,64]{3,2,1,0:T(8,128)(2,1)}, u32[]{:S(2)}) %copy-start.4) | copy-done | bytes 73752
  5.4 54.4 %shard_map.91 = bf16[64,32,128]{2,1,0:T(8,128)(2,1)S(1)} custom-call(bf16[64,32,128]{2,1,0:T(8,128)(2,1)S(1)} %copy-done, bf16[3,3,64,64]{3,2,1,0:T(8,128)(2,1)S(1)} %copy-done.1, f32[1,64]{1,0:T(1,128)S(1)} %bitcast.4, bf16[3,3,64,64]{3,2,1,0:T(8,128)(2,1)S(1)} %copy-done.2, f32[1,64]{1,0:T(1,128)S(1)} %bitcast.5, bf16[3,3,64,64]{3,2,1,0:T(8,128)(2,1)S(1)} %copy-done.3, ...), custom_call_target="tpu_custom_call" | custom-call | tf_op jit(solution)/shard_map/pallas_call | solution.py:511
  59.8 0.8 %copy.11 = bf16[64,32,128]{2,1,0:T(8,128)(2,1)} copy(bf16[64,32,128]{2,1,0:T(8,128)(2,1)S(1)} %shard_map.91) | data formatting | bytes 1048576
Async XLA Ops:
  0.0 0.7 %copy-start.8 = (f32[64]{0:T(128)S(1)}, f32[64]{0:T(128)}, u32[]{:S(2)}) copy-start(f32[64]{0:T(128)} %param.17) | copy-start | bytes 772
  0.0 0.7 %copy-start.5 = (f32[64]{0:T(128)S(1)}, f32[64]{0:T(128)}, u32[]{:S(2)}) copy-start(f32[64]{0:T(128)} %param.11) | copy-start | bytes 772
  0.0 0.7 %copy-start.6 = (f32[64]{0:T(128)S(1)}, f32[64]{0:T(128)}, u32[]{:S(2)}) copy-start(f32[64]{0:T(128)} %param.13) | copy-start | bytes 772
  0.0 0.7 %copy-start.7 = (f32[64]{0:T(128)S(1)}, f32[64]{0:T(128)}, u32[]{:S(2)}) copy-start(f32[64]{0:T(128)} %param.15) | copy-start | bytes 772
  0.7 1.0 %copy-start = (bf16[64,32,128]{2,1,0:T(8,128)(2,1)S(1)}, bf16[64,32,128]{2,1,0:T(8,128)(2,1)}, u32[]{:S(2)}) copy-start(bf16[64,32,128]{2,1,0:T(8,128)(2,1)} %x_hbm.1) | copy-start | bytes 1572868
  1.7 0.9 %copy-start.1 = (bf16[3,3,64,64]{3,2,1,0:T(8,128)(2,1)S(1)}, bf16[3,3,64,64]{3,2,1,0:T(8,128)(2,1)}, u32[]{:S(2)}) copy-start(bf16[3,3,64,64]{3,2,1,0:T(8,128)(2,1)} %k1a_hbm.1) | copy-start | bytes 221188
  2.7 0.9 %copy-start.2 = (bf16[3,3,64,64]{3,2,1,0:T(8,128)(2,1)S(1)}, bf16[3,3,64,64]{3,2,1,0:T(8,128)(2,1)}, u32[]{:S(2)}) copy-start(bf16[3,3,64,64]{3,2,1,0:T(8,128)(2,1)} %k1b_hbm.1) | copy-start | bytes 221188
  3.6 0.9 %copy-start.3 = (bf16[3,3,64,64]{3,2,1,0:T(8,128)(2,1)S(1)}, bf16[3,3,64,64]{3,2,1,0:T(8,128)(2,1)}, u32[]{:S(2)}) copy-start(bf16[3,3,64,64]{3,2,1,0:T(8,128)(2,1)} %k2a_hbm.1) | copy-start | bytes 221188
  4.5 0.9 %copy-start.4 = (bf16[3,3,64,64]{3,2,1,0:T(8,128)(2,1)S(1)}, bf16[3,3,64,64]{3,2,1,0:T(8,128)(2,1)}, u32[]{:S(2)}) copy-start(bf16[3,3,64,64]{3,2,1,0:T(8,128)(2,1)} %k2b_hbm.1) | copy-start | bytes 221188

commit v3 on v2

--- a/solution.py
+++ b/solution.py
@@ -267,9 +267,9 @@
 
     halo = Halo(4, frame, halo_send.at[0], halo_recv.at[0], halo_ss.at[0], halo_rs.at[0], row, col)
     halo.pack(ORDER)
+    prepare_one()
     pl.semaphore_wait(barrier, waits)
     halo.start()
-    prepare_one()
 
     everywhere, borders = ((0, 144),), ((0, 16), (128, 144))
 
@@ -435,6 +435,7 @@
                     frame[ROW_PAD + i, COL_PAD + j : COL_PAD + j + 16, :] = rounded(
                         (own + mirror[half]) * 0.5
                     )
+        shifted(4, ROW_PAD)(rows_at(t), 0)
         return 0
 
     halo = Halo(8, frame, halo_send.at[1], halo_recv.at[1], halo_ss.at[1], halo_rs.at[1], row, col)
@@ -442,10 +443,12 @@
     halo.pack(OTHERS, True)
     lax.fori_loop(SIDE // 2, SIDE, arrive, 0)
     halo.pack(SIDEWAYS, True)
+    lax.fori_loop(0, 2, conv_a(4, w2a, b2a, 4, 12), 0)
     halo.finish(OTHERS)
-
-    lax.fori_loop(0, 12, shifted(4, 0), 0)
-    lax.fori_loop(0, 2, conv_a(4, w2a, b2a, -4, 20), 0)
+    lax.fori_loop(0, 2, shifted(4, 0), 0)
+    lax.fori_loop(0, 2, shifted(4, ROW_PAD + 32), 0)
+    lax.fori_loop(0, 1, conv_a(4, w2a, b2a, -4, 8), 0)
+    lax.fori_loop(0, 1, conv_a(4, w2a, b2a, 28, 8), 0)
     halo.finish(SIDEWAYS)
     lax.fori_loop(0, 12, shifted(4, 0, borders), 0)
     lax.fori_loop(0, 1, conv_a(4, w2a, b2a, -4, 40, borders), 0)

time: 61.6 us -> 60.2 us (0.977); the launches traced: 60.6 us -> 60 us
    pallas_call x1, Pallas kernels: 54.4 us -> 53.8 us  [shards(): pl.pallas_call(body, out_shape=jax.ShapeDtypeStruct((CHAN, ROWS, COLS), B...]
where the time goes in v3:
time: 60.2 us; the launch traced here: 60 us
  Pallas kernels  53.8 us (89%)
  local copies, waits for them, and re-layouts  6.16 us (10%)
    pallas_call x1, Pallas kernels, shards(): pl.pallas_call(body, out_shape=jax.ShapeDtypeStruct((CHAN, ROWS, COLS), B...  53.8 us
    unnamed x19, local copies, waits for them, and re-layouts  6.16 us

profile of v3, /device:TPU:1, one launch (start us, length us, event | category | flops | bytes accessed | tf_op | source)
XLA Modules:
  0.0 60.0 jit_solution(1338728682273284274)
XLA Ops:
  0.0 0.0 copy-start.8
  0.0 0.0 copy-start.5
  0.0 0.0 copy-start.6
  0.0 0.0 copy-start.7
  0.0 0.6 %copy-done.8 = f32[64]{0:T(128)S(1)} copy-done((f32[64]{0:T(128)S(1)}, f32[64]{0:T(128)}, u32[]{:S(2)}) %copy-start.8) | copy-done | bytes 280
  0.7 0.0 copy-done.5
  0.7 0.0 copy-done.6
  0.7 0.0 copy-done.7
  0.7 0.0 copy-start
  0.7 1.0 %copy-done = bf16[64,32,128]{2,1,0:T(8,128)(2,1)S(1)} copy-done((bf16[64,32,128]{2,1,0:T(8,128)(2,1)S(1)}, bf16[64,32,128]{2,1,0:T(8,128)(2,1)}, u32[]{:S(2)}) %copy-start) | copy-done | bytes 524312
  1.7 0.0 copy-start.1
  1.7 0.9 %copy-done.1 = bf16[3,3,64,64]{3,2,1,0:T(8,128)(2,1)S(1)} copy-done((bf16[3,3,64,64]{3,2,1,0:T(8,128)(2,1)S(1)}, bf16[3,3,64,64]{3,2,1,0:T(8,128)(2,1)}, u32[]{:S(2)}) %copy-start.1) | copy-done | bytes 73752
  2.7 0.0 copy-start.2
  2.7 0.9 %copy-done.2 = bf16[3,3,64,64]{3,2,1,0:T(8,128)(2,1)S(1)} copy-done((bf16[3,3,64,64]{3,2,1,0:T(8,128)(2,1)S(1)}, bf16[3,3,64,64]{3,2,1,0:T(8,128)(2,1)}, u32[]{:S(2)}) %copy-start.2) | copy-done | bytes 73752
  3.6 0.0 copy-start.3
  3.6 0.9 %copy-done.3 = bf16[3,3,64,64]{3,2,1,0:T(8,128)(2,1)S(1)} copy-done((bf16[3,3,64,64]{3,2,1,0:T(8,128)(2,1)S(1)}, bf16[3,3,64,64]{3,2,1,0:T(8,128)(2,1)}, u32[]{:S(2)}) %copy-start.3) | copy-done | bytes 73752
  4.5 0.0 copy-start.4
  4.5 0.9 %copy-done.4 = bf16[3,3,64,64]{3,2,1,0:T(8,128)(2,1)S(1)} copy-done((bf16[3,3,64,64]{3,2,1,0:T(8,128)(2,1)S(1)}, bf16[3,3,64,64]{3,2,1,0:T(8,128)(2,1)}, u32[]{:S(2)}) %copy-start.4) | copy-done | bytes 73752
  5.4 53.8 %shard_map.91 = bf16[64,32,128]{2,1,0:T(8,128)(2,1)S(1)} custom-call(bf16[64,32,128]{2,1,0:T(8,128)(2,1)S(1)} %copy-done, bf16[3,3,64,64]{3,2,1,0:T(8,128)(2,1)S(1)} %copy-done.1, f32[1,64]{1,0:T(1,128)S(1)} %bitcast.4, bf16[3,3,64,64]{3,2,1,0:T(8,128)(2,1)S(1)} %copy-done.2, f32[1,64]{1,0:T(1,128)S(1)} %bitcast.5, bf16[3,3,64,64]{3,2,1,0:T(8,128)(2,1)S(1)} %copy-done.3, ...), custom_call_target="tpu_custom_call" | custom-call | tf_op jit(solution)/shard_map/pallas_call | solution.py:514
  59.2 0.8 %copy.11 = bf16[64,32,128]{2,1,0:T(8,128)(2,1)} copy(bf16[64,32,128]{2,1,0:T(8,128)(2,1)S(1)} %shard_map.91) | data formatting | bytes 1048576
Async XLA Ops:
  0.0 0.7 %copy-start.8 = (f32[64]{0:T(128)S(1)}, f32[64]{0:T(128)}, u32[]{:S(2)}) copy-start(f32[64]{0:T(128)} %param.17) | copy-start | bytes 772
  0.0 0.7 %copy-start.5 = (f32[64]{0:T(128)S(1)}, f32[64]{0:T(128)}, u32[]{:S(2)}) copy-start(f32[64]{0:T(128)} %param.11) | copy-start | bytes 772
  0.0 0.7 %copy-start.6 = (f32[64]{0:T(128)S(1)}, f32[64]{0:T(128)}, u32[]{:S(2)}) copy-start(f32[64]{0:T(128)} %param.13) | copy-start | bytes 772
  0.0 0.7 %copy-start.7 = (f32[64]{0:T(128)S(1)}, f32[64]{0:T(128)}, u32[]{:S(2)}) copy-start(f32[64]{0:T(128)} %param.15) | copy-start | bytes 772
  0.7 1.0 %copy-start = (bf16[64,32,128]{2,1,0:T(8,128)(2,1)S(1)}, bf16[64,32,128]{2,1,0:T(8,128)(2,1)}, u32[]{:S(2)}) copy-start(bf16[64,32,128]{2,1,0:T(8,128)(2,1)} %x_hbm.1) | copy-start | bytes 1572868
  1.7 0.9 %copy-start.1 = (bf16[3,3,64,64]{3,2,1,0:T(8,128)(2,1)S(1)}, bf16[3,3,64,64]{3,2,1,0:T(8,128)(2,1)}, u32[]{:S(2)}) copy-start(bf16[3,3,64,64]{3,2,1,0:T(8,128)(2,1)} %k1a_hbm.1) | copy-start | bytes 221188
  2.7 0.9 %copy-start.2 = (bf16[3,3,64,64]{3,2,1,0:T(8,128)(2,1)S(1)}, bf16[3,3,64,64]{3,2,1,0:T(8,128)(2,1)}, u32[]{:S(2)}) copy-start(bf16[3,3,64,64]{3,2,1,0:T(8,128)(2,1)} %k1b_hbm.1) | copy-start | bytes 221188
  3.6 0.9 %copy-start.3 = (bf16[3,3,64,64]{3,2,1,0:T(8,128)(2,1)S(1)}, bf16[3,3,64,64]{3,2,1,0:T(8,128)(2,1)}, u32[]{:S(2)}) copy-start(bf16[3,3,64,64]{3,2,1,0:T(8,128)(2,1)} %k2a_hbm.1) | copy-start | bytes 221188
  4.5 0.9 %copy-start.4 = (bf16[3,3,64,64]{3,2,1,0:T(8,128)(2,1)S(1)}, bf16[3,3,64,64]{3,2,1,0:T(8,128)(2,1)}, u32[]{:S(2)}) copy-start(bf16[3,3,64,64]{3,2,1,0:T(8,128)(2,1)} %k2b_hbm.1) | copy-start | bytes 221188
